TPU v7x, 128 devices: a whole 4x4x4 slice. The times are simulated.
128 devices in a mesh: cube: 8 (over x_hi, z), front: 16 (over y, x_lo, core).
Axes of the slice: x: 4 (x_hi: 2, x_lo: 2; x = x_hi * 2 + x_lo), y: 4, z: 4, core: 2. Of those that a mesh axis runs over, the one named last changes fastest.
Arguments:
- child_block: float32 [8, 16, 14, 128, 512], P('cube', 'front'), may hold values from -4 to 4, as said below
- child_rows: int32 [8, 16, 14], P('cube', 'front'), may hold values from 0 to 255, as said below
- child_cols: int32 [8, 4], P('cube'), may hold values from 0 to 5, as said below
- parent_base: float32 [8, 16, 8, 128, 768], P('cube', 'front'), may hold values from -16 to 36, as said below
Outputs:
- lower_factor: float32 [8, 16, 8, 128, 768], P('cube', 'front')
Inputs may be any that keep to these rules, and one draw needn't show every extreme that they name: `child_rows`: group g's child feeds the front of pair g // 2. The 14 tiles at front index f go to distinct increasing parent tiles within 2 * 16 * (f % 8) to 2 * 16 * (f % 8 + 1) - 1; each child's first tile goes to 0 and its last to 255. `child_cols`: distinct and increasing for each group; the first is 0 and the last 5. `child_block`: rows of tiles that go to parent tiles under 6 lie within -0.005 to 0.005. `parent_base`: the first 768 rows of each front form a symmetric matrix whose smallest eigenvalue is 10 or more.
All inputs are finite; a program needn't handle non-finite values.
Results may differ from a plain program's by a relative error of at most 0.0001.
Values sent between devices are 32-bit elements; how exact they have to be, the bound alone decides.
A program may use at most 128 MiB of HBM per device.

v0:
```python
import jax
import jax.numpy as jnp
from jax import lax
from jax.sharding import PartitionSpec as P


def partner(block, axis, apart):
    count = lax.axis_size(axis)
    route = []
    for low in range(count):
        high = low | 1 << apart
        if high != low and high < count:
            route += [(low, high), (high, low)]
    return lax.ppermute(block, axis, route)


def widen_cols(child_data, col_map, win_tiles):
    leading = child_data.shape[:-1]
    col_tiles = col_map.shape[0]
    tile_rows = child_data.shape[-2]
    placer = (col_map[:, None] == jnp.arange(win_tiles, dtype=jnp.int32)[None, :]).astype(
        jnp.float32
    )
    split_cols = child_data.reshape(leading + (col_tiles, tile_rows))
    widened = jnp.einsum("...cq,cw->...wq", split_cols, placer, precision=lax.Precision.HIGHEST)
    return widened.reshape(leading + (win_tiles * tile_rows,))


def body(child_block, child_rows, child_cols, parent_base):
    fronts = lax.axis_size("front")
    rtiles = parent_base.shape[2]
    tile_rows = parent_base.shape[3]
    window = parent_base.shape[4]
    win_tiles = window // tile_rows
    panel_cols = 2 * tile_rows
    panels = window // panel_cols
    my_bit = lax.axis_index("cube") % 2
    my_front = lax.axis_index("front")
    own_block = child_block[0, 0]
    rows_map = child_rows[0, 0]
    cols_map = child_cols[0]
    owners = rows_map % (2 * fronts)
    dest_bit = owners % 2
    dest_front = owners // 2
    slot_index = rows_map // (2 * fronts)
    bit_ids = jnp.arange(2, dtype=jnp.int32)
    front_ids = jnp.arange(fronts, dtype=jnp.int32)
    hits = (dest_bit[:, None, None] == bit_ids[None, :, None]) & (
        dest_front[:, None, None] == front_ids[None, None, :]
    )
    routing = hits.astype(jnp.float32)
    labels = jnp.sum(hits.astype(jnp.int32) * (slot_index + 1)[:, None, None], axis=0)
    staying_labels = lax.dynamic_index_in_dim(labels, my_bit, 0, keepdims=False)
    leaving_labels = lax.dynamic_index_in_dim(labels, 1 - my_bit, 0, keepdims=False)
    payload = widen_cols(own_block, cols_map, win_tiles)
    outgoing = jnp.einsum("tbf,trc->bfrc", routing, payload, precision=lax.Precision.HIGHEST)
    staying = lax.dynamic_index_in_dim(outgoing, my_bit, 0, keepdims=False)
    leaving = lax.dynamic_index_in_dim(outgoing, 1 - my_bit, 0, keepdims=False)
    sibling_data, sibling_labels = partner((leaving, leaving_labels), "cube", 0)
    combined = jnp.stack([staying, sibling_data], axis=1)
    combined_labels = jnp.stack([staying_labels, sibling_labels], axis=1)
    arrived, arrived_labels = (
        lax.all_to_all(combined, "front", split_axis=0, concat_axis=0, tiled=True),
        lax.all_to_all(combined_labels, "front", split_axis=0, concat_axis=0, tiled=True),
    )
    local_ids = jnp.arange(rtiles, dtype=jnp.int32)
    landing = (arrived_labels.reshape(-1)[:, None] == (local_ids + 1)[None, :]).astype(jnp.float32)
    added = jnp.einsum(
        "sj,src->jrc",
        landing,
        arrived.reshape((2 * fronts, tile_rows, window)),
        precision=lax.Precision.HIGHEST,
    )
    assembled = (parent_base[0, 0] + added).reshape(rtiles * tile_rows, window)
    row_index = (
        (local_ids[:, None] * (2 * fronts) + 2 * my_front + my_bit) * tile_rows
        + jnp.arange(tile_rows, dtype=jnp.int32)[None, :]
    ).reshape(-1)
    for panel_id in range(panels):
        col_start = panel_id * panel_cols
        col_stop = col_start + panel_cols
        top_tile = assembled[:tile_rows, col_start:col_stop]
        gathered = lax.all_gather(top_tile, "front", axis=0, tiled=True)
        local_rows = gathered[: panels * tile_rows]
        partner_rows = partner(local_rows, "cube", 0)
        bit_zero = jnp.where(my_bit == 0, local_rows, partner_rows).reshape(
            panels, tile_rows, panel_cols
        )
        bit_one = jnp.where(my_bit == 0, partner_rows, local_rows).reshape(
            panels, tile_rows, panel_cols
        )
        win_rows = jnp.stack([bit_zero, bit_one], axis=1).reshape(win_tiles * tile_rows, panel_cols)
        factor = jnp.linalg.cholesky(win_rows[col_start:col_stop])
        local_panel = lax.linalg.triangular_solve(
            factor, assembled[:, col_start:col_stop], left_side=False, lower=True, transpose_a=True
        )
        factor_rows = factor[jnp.clip(row_index - col_start, 0, panel_cols - 1)]
        under = row_index[:, None] >= col_stop
        inside = row_index[:, None] >= col_start
        new_panel = jnp.where(under, local_panel, jnp.where(inside, factor_rows, 0.0))
        assembled = assembled.at[:, col_start:col_stop].set(new_panel)
        if col_stop < window:
            below = lax.linalg.triangular_solve(
                factor, win_rows[col_stop:], left_side=False, lower=True, transpose_a=True
            )
            update = jnp.dot(
                jnp.where(under, local_panel, 0.0), below.T, precision=lax.Precision.HIGHEST
            )
            assembled = assembled.at[:, col_stop:].add(-update)
    return assembled.reshape(1, 1, rtiles, tile_rows, window)


def solution(mesh):
    placed = (
        P("cube", "front", None, None, None),
        P("cube", "front", None),
        P("cube", None),
        P("cube", "front", None, None, None),
    )
    return jax.shard_map(
        body,
        mesh=mesh,
        in_specs=placed,
        out_specs=P("cube", "front", None, None, None),
        check_vma=False,
    )
```

profile of v0, /device:TPU:31, one launch (start us, length us, event | category | flops | bytes accessed | tf_op | source)
XLA Modules:
  0.0 880.0 jit_solution(13228059308978961303)
XLA Ops:
  34.5 12.3 %fusion = f32[2,16,128,768]{3,1,2,0:T(8,128)} fusion(f32[14,128,768]{2,0,1:T(8,128)} %copy.84, pred[14,16]{0,1:T(8,128)(4,1)S(1)} %iota_compare_fusion.3, pred[14,2]{0,1:T(4,128)(4,1)S(1)} %iota_compare_fusion.5), kind=kOutput, calls=%fused_computation.10 | convolution fusion | flops 528482752 | bytes 18088188 | tf_op jit(solution)/shard_map/tbf,trc->bfrc/dot_general | solution.py:56
  55.2 9.1 %copy.129 = f32[1,16,128,768]{3,2,1,0:T(8,128)} copy(f32[1,16,128,768]{3,1,2,0:T(8,128)} %get-tuple-element.147) | data formatting | bytes 12582912 | tf_op jit(solution)/shard_map/jit(dynamic_index_in_dim)/dynamic_slice | solution.py:58
  72.4 128.9 %collective-permute-done = s32[16]{0:T(128)S(1)} collective-permute-done((s32[16]{0:T(128)S(1)}, s32[16]{0:T(128)S(1)}, u32[]{:S(2)}, u32[]{:S(2)}) %collective-permute-start) | collective-permute-done | bytes 96 | tf_op jit(solution)/shard_map/ppermute | solution.py:14
  208.9 10.5 %pad_maximum_fusion = f32[16,2,128,768]{3,2,0,1:T(8,128)} fusion(f32[16,1,128,768]{3,2,0,1:T(8,128)} %bitcast.17, f32[16,1,128,768]{3,2,0,1:T(8,128)} %bitcast.200), kind=kLoop, calls=%fused_computation.9 | loop fusion | flops 3145728 | bytes 25165824 | tf_op jit(solution)/shard_map/stack | solution.py:60
  219.4 22.1 %copy.87 = f32[16,2,128,768]{3,1,2,0:T(2,128)} copy(f32[16,2,128,768]{3,2,0,1:T(8,128)} %pad_maximum_fusion) | data formatting | bytes 25165824 | tf_op jit(solution)/shard_map/stack | solution.py:60
  248.6 135.2 %all-to-all-done.1 = f32[16,2,128,768]{3,1,2,0:T(2,128)} async-done(((f32[16,2,128,768]{3,1,2,0:T(2,128)}), f32[16,2,128,768]{3,1,2,0:T(2,128)}, u32[]{:S(2)}, u32[]{:S(2)}) %all-to-all-start.1) | async-done | bytes 12582944 | tf_op jit(solution)/shard_map/all_to_all | solution.py:63
  383.8 11.6 %copy.88 = f32[16,2,128,768]{3,1,0,2:T(2,128)} copy(f32[16,2,128,768]{3,1,2,0:T(2,128)} %all-to-all-done.1) | data formatting | bytes 25165824 | tf_op jit(solution)/shard_map/all_to_all | solution.py:63
  395.5 15.9 %reshape.460 = f32[32,128,768]{2,0,1:T(8,128)} reshape(f32[16,2,128,768]{3,1,0,2:T(2,128)} %copy.88) | data formatting | bytes 25165824 | tf_op jit(solution)/shard_map/reshape | solution.py:71
  427.5 38.1 %all-gather.4.cloned.1.call-done = f32[2048,256]{0,1:T(8,128)} async-done(((f32[128,256]{0,1:T(8,128)}), f32[2048,256]{0,1:T(8,128)}) %all-gather.4.cloned.1.call-update) | async-done | bytes 2097168 | tf_op jit(solution)/shard_map/all_gather | solution.py:83
  488.5 11.7 %cholesky.172 = f32[128,128]{1,0:T(8,128)S(1)} custom-call(f32[128,128]{1,0:T(8,128)S(1)} %cholesky.270), custom_call_target="Cholesky" | custom-call | tf_op jit(solution)/shard_map/jit(cholesky)/cholesky | solution.py:93
  500.9 9.8 %custom-call.23 = f32[1,128,128]{1,2,0:T(8,128)S(1)} custom-call(f32[1,128,128]{2,1,0:T(8,128)S(1)} %get-tuple-element.167), custom_call_target="InvertDiagBlocksLowerTriangular" | custom-call | tf_op jit(solution)/shard_map/jit(cholesky)/cholesky | solution.py:93
  512.8 11.7 %cholesky.189 = f32[128,128]{1,0:T(8,128)S(1)} custom-call(f32[128,128]{1,0:T(8,128)S(1)} %convolution_subtract_fusion.7), custom_call_target="Cholesky" | custom-call | tf_op jit(solution)/shard_map/jit(cholesky)/cholesky | solution.py:93
  538.3 20.5 %custom-call.24 = f32[2,128,128]{1,2,0:T(8,128)S(1)} custom-call(f32[2,128,128]{2,1,0:T(8,128)} %copy-done.21), custom_call_target="InvertDiagBlocksLowerTriangular" | custom-call | tf_op jit(solution)/shard_map/triangular_solve/custom-call.0 | solution.py:94
  582.4 38.4 %all-gather.6.cloned.1.call-done = f32[2048,256]{0,1:T(8,128)} async-done(((f32[128,256]{0,1:T(8,128)}), f32[2048,256]{0,1:T(8,128)}) %all-gather.6.cloned.1.call-update) | async-done | bytes 2097168 | tf_op jit(solution)/shard_map/all_gather | solution.py:83
  623.4 9.2 %collective-permute-done.3 = f32[384,256]{0,1:T(8,128)S(1)} collective-permute-done((f32[384,256]{0,1:T(8,128)S(1)}, f32[384,256]{0,1:T(8,128)S(1)}, u32[]{:S(2)}, u32[]{:S(2)}) %collective-permute-start.3) | collective-permute-done | bytes 393248 | tf_op jit(solution)/shard_map/ppermute | solution.py:14
  642.7 11.7 %cholesky.206 = f32[128,128]{1,0:T(8,128)S(1)} custom-call(f32[128,128]{1,0:T(8,128)S(1)} %cholesky.273), custom_call_target="Cholesky" | custom-call | tf_op jit(solution)/shard_map/jit(cholesky)/cholesky | solution.py:93
  654.5 9.8 %custom-call.25 = f32[1,128,128]{1,2,0:T(8,128)S(1)} custom-call(f32[1,128,128]{2,1,0:T(8,128)S(1)} %get-tuple-element.163), custom_call_target="InvertDiagBlocksLowerTriangular" | custom-call | tf_op jit(solution)/shard_map/jit(cholesky)/cholesky | solution.py:93
  666.4 11.7 %cholesky.223 = f32[128,128]{1,0:T(8,128)S(1)} custom-call(f32[128,128]{1,0:T(8,128)S(1)} %convolution_subtract_fusion.6), custom_call_target="Cholesky" | custom-call | tf_op jit(solution)/shard_map/jit(cholesky)/cholesky | solution.py:93
  690.7 20.5 %custom-call.26 = f32[2,128,128]{1,2,0:T(8,128)S(1)} custom-call(f32[2,128,128]{2,1,0:T(8,128)} %copy-done.22), custom_call_target="InvertDiagBlocksLowerTriangular" | custom-call | tf_op jit(solution)/shard_map/triangular_solve/custom-call.0 | solution.py:94
  734.3 38.5 %all-gather.8.cloned.1.call-done = f32[2048,256]{0,1:T(8,128)} async-done(((f32[128,256]{0,1:T(8,128)}), f32[2048,256]{0,1:T(8,128)}) %all-gather.8.cloned.1.call-update) | async-done | bytes 2097168 | tf_op jit(solution)/shard_map/all_gather | solution.py:83
  793.9 11.7 %cholesky.240 = f32[128,128]{1,0:T(8,128)S(1)} custom-call(f32[128,128]{1,0:T(8,128)S(1)} %cholesky.276), custom_call_target="Cholesky" | custom-call | tf_op jit(solution)/shard_map/jit(cholesky)/cholesky | solution.py:93
  805.7 9.8 %custom-call.27 = f32[1,128,128]{1,2,0:T(8,128)S(1)} custom-call(f32[1,128,128]{2,1,0:T(8,128)S(1)} %get-tuple-element.159), custom_call_target="InvertDiagBlocksLowerTriangular" | custom-call | tf_op jit(solution)/shard_map/jit(cholesky)/cholesky | solution.py:93
  817.6 11.7 %cholesky.257 = f32[128,128]{1,0:T(8,128)S(1)} custom-call(f32[128,128]{1,0:T(8,128)S(1)} %convolution_subtract_fusion.5), custom_call_target="Cholesky" | custom-call | tf_op jit(solution)/shard_map/jit(cholesky)/cholesky | solution.py:93
  846.6 19.7 %custom-call.28 = f32[2,128,128]{1,2,0:T(8,128)S(1)} custom-call(f32[2,128,128]{2,1,0:T(8,128)S(1)} %get-tuple-element.105), custom_call_target="InvertDiagBlocksLowerTriangular" | custom-call | tf_op jit(solution)/shard_map/triangular_solve/custom-call.0 | solution.py:94
  (214 shorter events, 251.7 us)
Async XLA Ops:
  7.3 5.1 copy-start.28
  64.3 144.6 %collective-permute-start.1 = (f32[16,128,768]{2,1,0:T(8,128)}, f32[16,128,768]{2,1,0:T(8,128)}, u32[]{:S(2)}, u32[]{:S(2)}) collective-permute-start(f32[16,128,768]{2,1,0:T(8,128)} %bitcast.180), channel_id=1, source_target_pairs={{0,16},{16,0},{32,48},{48,32},{64,80},{80,64},{96,112},{112,96},{1... | collective-permute-start | bytes 18874376 | tf_op jit(solution)/shard_map/ppermute | solution.py:14
  66.1 135.3 %collective-permute-start = (s32[16]{0:T(128)S(1)}, s32[16]{0:T(128)S(1)}, u32[]{:S(2)}, u32[]{:S(2)}) collective-permute-start(s32[16]{0:T(128)S(1)} %get-tuple-element.169), channel_id=1, source_target_pairs={{0,16},{16,0},{32,48},{48,32},{64,80},{80,64},{96,112},{112,96},{1... | collective-permute-start | bytes 200 | tf_op jit(solution)/shard_map/ppermute | solution.py:14
  202.0 39.5 %all-to-all-start = ((s32[16,1,2]{2,1,0:T(1,128)}), s32[16,1,2]{2,1,0:T(1,128)S(1)}, u32[]{:S(2)}, u32[]{:S(2)}) async-start(s32[16,1,2]{2,1,0:T(1,128)} %copy.82), calls=%async_computation | async-start | bytes 16384 | tf_op jit(solution)/shard_map/all_to_all | solution.py:64
  241.5 142.3 %all-to-all-start.1 = ((f32[16,2,128,768]{3,1,2,0:T(2,128)}), f32[16,2,128,768]{3,1,2,0:T(2,128)}, u32[]{:S(2)}, u32[]{:S(2)}) async-start(f32[16,2,128,768]{3,1,2,0:T(2,128)} %copy.87), calls=%async_computation.1 | async-start | bytes 25165824 | tf_op jit(solution)/shard_map/all_to_all | solution.py:63
  247.3 218.3 %all-gather.4.cloned.1.call-start = ((), (), s32[]{:S(2)}) async-start(), calls=%async_computation.2 | async-start | bytes 2228224 | tf_op jit(solution)/shard_map/all_gather | solution.py:83
  395.5 15.9 %copy-start.9 = (f32[1,1,8,128,768]{4,3,2,1,0:T(8,128)S(1)}, f32[1,1,8,128,768]{4,3,2,1,0:T(8,128)}, u32[]{:S(2)}) copy-start(f32[1,1,8,128,768]{4,3,2,1,0:T(8,128)} %param.20) | copy-start | bytes 9437188
  426.1 194.7 %all-gather.6.cloned.1.call-start = ((), (), s32[]{:S(2)}) async-start(), calls=%async_computation.3 | async-start | bytes 2228224 | tf_op jit(solution)/shard_map/all_gather | solution.py:83
  466.6 10.7 %collective-permute-start.2 = (f32[384,256]{0,1:T(8,128)S(1)}, f32[384,256]{0,1:T(8,128)S(1)}, u32[]{:S(2)}, u32[]{:S(2)}) collective-permute-start(f32[384,256]{0,1:T(8,128)S(1)} %slice.299), channel_id=1, source_target_pairs={{0,16},{16,0},{32,48},{48,32},{64,80},{80,64},{96,112},{112,96},{1... | collective-permute-start | bytes 1179656 | tf_op jit(solution)/shard_map/ppermute | solution.py:14
  468.8 108.6 %copy-start.24 = (pred[1024]{0:T(1024)(128)(4,1)}, pred[1024]{0:T(1024)(128)(4,1)S(1)}, u32[]{:S(2)}) copy-start(pred[1024]{0:T(1024)(128)(4,1)S(1)} %get-tuple-element.173) | copy-start | bytes 3076
  559.5 5.0 copy-start.4
  567.4 7.3 copy-start.27
  572.1 5.4 copy-start.11
  574.6 2.8 copy-start.12
  582.3 190.4 %all-gather.8.cloned.1.call-start = ((), (), s32[]{:S(2)}) async-start(), calls=%async_computation.4 | async-start | bytes 2228224 | tf_op jit(solution)/shard_map/all_gather | solution.py:83
  621.8 10.7 %collective-permute-start.3 = (f32[384,256]{0,1:T(8,128)S(1)}, f32[384,256]{0,1:T(8,128)S(1)}, u32[]{:S(2)}, u32[]{:S(2)}) collective-permute-start(f32[384,256]{0,1:T(8,128)S(1)} %slice.308), channel_id=1, source_target_pairs={{0,16},{16,0},{32,48},{48,32},{64,80},{80,64},{96,112},{112,96},{1... | collective-permute-start | bytes 1179656 | tf_op jit(solution)/shard_map/ppermute | solution.py:14
  712.9 4.6 copy-start.2
  721.4 7.3 copy-start.23
  721.4 7.3 copy-start.25
  726.1 5.4 copy-start.20
  773.8 10.8 %collective-permute-start.4 = (f32[384,256]{0,1:T(8,128)S(1)}, f32[384,256]{0,1:T(8,128)S(1)}, u32[]{:S(2)}, u32[]{:S(2)}) collective-permute-start(f32[384,256]{0,1:T(8,128)S(1)} %slice.317), channel_id=1, source_target_pairs={{0,16},{16,0},{32,48},{48,32},{64,80},{80,64},{96,112},{112,96},{1... | collective-permute-start | bytes 1179656 | tf_op jit(solution)/shard_map/ppermute | solution.py:14
  833.6 7.5 copy-start.29
  838.5 31.9 %copy-start.26 = (pred[1024]{0:T(1024)(128)(4,1)S(1)}, pred[1024]{0:T(1024)(128)(4,1)}, u32[]{:S(2)}) copy-start(pred[1024]{0:T(1024)(128)(4,1)} %get-tuple-element.170) | copy-start | bytes 3076
  866.3 4.1 copy-start.8
  (16 other events, 27.1 us)
Sparse Core Ops, SparseCore 0:
  426.2 39.3 all-gather.3
  582.5 38.2 all-gather.5
  734.4 38.2 all-gather.7
where the time goes:
time: 891 us; the launch traced here: 880 us
  waiting for transfers between devices  405 us (45%)
  other arithmetic  204 us (23%)
  local copies, waits for them, and re-layouts  172 us (19%)
  matrix products  61.6 us (7%)
  starting transfers between devices  19.1 us (2%)
  between operations  18 us (2%)
    ppermute x5, waiting for transfers between devices, partner(): return lax.ppermute(block, axis, route)  154 us
    all_to_all x1, waiting for transfers between devices, body(): lax.all_to_all(combined, 'front', split_axis=0, concat_axis=0, tiled=True)  135 us
    all_gather x3, waiting for transfers between devices, body(): gathered = lax.all_gather(top_tile, 'front', axis=0, tiled=True)  115 us
    another operation x20, other arithmetic, body(): factor = jnp.linalg.cholesky(win_rows[col_start:col_stop])  104 us
    another operation x7, other arithmetic, body(): lax.linalg.triangular_solve(factor, assembled[:, col_start:col_stop], lef...  66.2 us
    another operation x1, local copies, waits for them, and re-layouts, body(): combined = jnp.stack([staying, sibling_data], axis=1)  22.1 us
    gather x6, local copies, waits for them, and re-layouts, body(): factor_rows = factor[jnp.clip(row_index - col_start, 0, panel_cols - 1)]  22 us
    another operation x22, local copies, waits for them, and re-layouts, body(): lax.linalg.triangular_solve(factor, assembled[:, col_start:col_stop], lef...  21 us
  transfers between devices with their start and end apart: 10, of which 8 were waited for; matrix products, arithmetic and copies ran while one was open for 5% of the time, Pallas kernels for 0%

commit v1 on v0

v1 whole, which is shorter than its diff:
```python
import functools

import jax
import jax.numpy as jnp
from jax import lax
from jax.experimental import pallas as pl
from jax.experimental.pallas import tpu as pltpu
from jax.sharding import Mesh
from jax.sharding import PartitionSpec as P

MESH = pl.DeviceIdType.MESH
HI = lax.Precision.HIGHEST
VM = pl.BlockSpec(memory_space=pltpu.VMEM)
ANY = pl.BlockSpec(memory_space=pl.ANY)
def nt(a,b,prec=HI):
    return lax.dot_general(a,b,(((1,),(1,)),((),())),precision=prec,preferred_element_type=jnp.float32)
def nn(a,b,prec=HI):
    return lax.dot_general(a,b,(((1,),(0,)),((),())),precision=prec,preferred_element_type=jnp.float32)
def bc(x): return jnp.broadcast_to(x,(8,128))
def base(block):
    sub=lax.broadcasted_iota(jnp.int32,(8,128),0); lane=lax.broadcasted_iota(jnp.int32,(8,128),1)
    S=[block[8*t:8*t+8] for t in range(16)]
    T=[jnp.where(lane==sub+8*t,1.0,0.0).astype(jnp.float32) for t in range(16)]
    U=[];M=[]
    for s in range(16):
        ur=[];mr=[]
        for r in range(0,8,2):
            i=8*s+r
            R=S[s]; Q=T[s]
            c0=bc(R[:,i:i+1]); c1=bc(R[:,i+1:i+2])
            a=bc(c0[r:r+1]); b=bc(c0[r+1:r+2]); c=bc(c1[r+1:r+2])
            w0=bc(R[r:r+1]); w1=bc(R[r+1:r+2]); t0=bc(Q[r:r+1]); t1=bc(Q[r+1:r+2])
            rd=1.0/(a*c-b*b)
            A=c*rd; B=b*rd; C=a*rd
            for t in range(s,16):
                if t>s:
                    c0=bc(S[t][:,i:i+1]); c1=bc(S[t][:,i+1:i+2])
                elif r==6: continue
                else:
                    keep=sub>r+1
                    c0=jnp.where(keep,c0,0.0); c1=jnp.where(keep,c1,0.0)
                e0=c0*A-c1*B; e1=c1*C-c0*B
                S[t]=S[t]-(e0*w0+e1*w1)
                T[t]=T[t]-(e0*t0+e1*t1)
            ra=lax.rsqrt(a); q=b*(ra*ra); rs=lax.rsqrt(c-b*q)
            ur+=[w0*ra,(w1-q*w0)*rs]; mr+=[t0*ra,(t1-q*t0)*rs]
        def merge(rows):
            o=rows[7]
            for k in range(7): o=jnp.where(sub==k,rows[k],o)
            return o
        U.append(merge(ur)); M.append(merge(mr))
    return jnp.concatenate(U,0), jnp.concatenate(M,0)
NB=6
def chol_kernel(a_ref, l_ref, m_ref, w_ref):
    def blk(i,j): return (pl.ds(128*i,128),pl.ds(128*j,128))
    for i in range(NB):
        for j in range(i+1):
            v=a_ref[blk(i,j)]
            if i//2==j//2:
                v=0.5*(v+(v.T if i==j else a_ref[blk(j,i)].T))
            w_ref[blk(i,j)]=v
    tri=lax.broadcasted_iota(jnp.int32,(128,128),0)>=lax.broadcasted_iota(jnp.int32,(128,128),1)
    zero=jnp.zeros((128,128),jnp.float32)
    for k in range(NB):
        U,M=base(w_ref[blk(k,k)])
        l_ref[blk(k,k)]=jnp.where(tri,U.T,0.0)
        m_ref[blk(k,k)]=M
        for j in range(k+1,NB):
            l_ref[blk(k,j)]=zero; m_ref[blk(k,j)]=zero
        if k+1<NB:
            n=128*(NB-1-k); r0=128*(k+1)
            P=nt(w_ref[pl.ds(r0,n),pl.ds(128*k,128)],M)
            l_ref[pl.ds(r0,n),pl.ds(128*k,128)]=P
            for j in range(k+1,NB):
                q0=128*(j-k-1)
                w_ref[pl.ds(128*j,n-q0),pl.ds(128*j,128)]-=nt(P[q0:],P[q0:q0+128])
        if k>0:
            acc=nn(l_ref[pl.ds(128*k,128),pl.ds(0,128*k)],m_ref[pl.ds(0,128*k),pl.ds(0,128*k)])
            m_ref[pl.ds(128*k,128),pl.ds(0,128*k)]=-nn(M,acc)
def chol(top):
    s = jax.ShapeDtypeStruct((768, 768), jnp.float32)
    return pl.pallas_call(
        chol_kernel,
        out_shape=(s, s),
        in_specs=[VM],
        out_specs=(VM, VM),
        scratch_shapes=[pltpu.VMEM((768, 768), jnp.float32)],
        compiler_params=pltpu.CompilerParams(vmem_limit_bytes=40 << 20),
        cost_estimate=pl.CostEstimate(flops=40_000_000_000, bytes_accessed=8_000_000, transcendentals=0),
        name="lead_factor",
    )(top)


def pack_kernel(pick, x_ref, o_ref):
    d = pl.program_id(0)
    o_ref[...] = jnp.where(pick[d] > 0, x_ref[...], 0.0)


def pack(pick, tiles):
    block = (1, 128, 512)
    return pl.pallas_call(
        pack_kernel,
        out_shape=jax.ShapeDtypeStruct((32, 128, 512), jnp.float32),
        grid_spec=pltpu.PrefetchScalarGridSpec(
            num_scalar_prefetch=1,
            grid=(32,),
            in_specs=[pl.BlockSpec(block, lambda d, pick: (jnp.maximum(pick[d] - 1, 0), 0, 0))],
            out_specs=pl.BlockSpec(block, lambda d, pick: (d, 0, 0)),
        ),
        name="pack_tiles",
    )(pick, tiles)


def spread(w, g, s, col):
    if col == 0:
        return s(0)
    if col == 5:
        return s(3)
    if col == 1:
        return s(1) * w[g, 0:1]
    if col == 2:
        return s(1) * w[g, 1:2] + s(2) * w[g, 2:3]
    if col == 3:
        return s(1) * w[g, 3:4] + s(2) * w[g, 4:5]
    return s(2) * w[g, 5:6]


def top_kernel(packed, base_tiles, w_in, top, wb, cbuf, bbuf, ssem, wsem, csem, bsem, ysem, xsem, ksem):
    pair = lax.axis_index("pair")
    z = lax.axis_index("bit")
    f = lax.axis_index("front")
    y, x, k = f // 4, (f // 2) % 2, f % 2

    def at(dz, dy, dx, dk):
        return (pair, (z + dz) % 2, ((y + dy) % 4) * 4 + ((x + dx) % 2) * 2 + (k + dk) % 2)

    bar = pltpu.get_barrier_semaphore()
    for n in range(1, 32):
        pl.semaphore_signal(bar, inc=1, device_id=at(n // 16, (n // 4) % 4, (n // 2) % 2, n % 2), device_id_type=MESH)
    pl.semaphore_wait(bar, 31)

    wb[z] = w_in[...]
    wcopy = pltpu.make_async_remote_copy(
        src_ref=w_in, dst_ref=wb.at[z], send_sem=wsem.at[0], recv_sem=wsem.at[1],
        device_id=at(1, 0, 0, 0), device_id_type=MESH)
    wcopy.start()
    owner = f <= 2
    source = (f == 0) | (f == 8)
    me = z * 2 + y // 2
    widths = (256, 384, 512)

    def child(b, q, remote):
        src = packed.at[b * 16 + q, :, pl.ds(0, widths[q])]
        dst = cbuf.at[me, :, pl.ds(0, widths[q])]
        if remote:
            return pltpu.make_async_remote_copy(
                src_ref=src, dst_ref=dst, send_sem=ssem.at[b * 3 + q], recv_sem=csem.at[me],
                device_id=(pair, b, q), device_id_type=MESH)
        return pltpu.make_async_copy(src, dst, csem.at[me])

    def each(fn):
        for q in range(3):
            for b in range(2):
                if q == 0:
                    own = (f == 0) & (z == b)
                    fn(b, q, source & jnp.logical_not(own), True)
                    if fn is begin:
                        fn(b, q, source & own, False)
                else:
                    fn(b, q, source, True)

    def begin(b, q, cond, remote):
        @pl.when(cond)
        def _():
            child(b, q, remote).start()

    def sent(b, q, cond, remote):
        @pl.when(cond)
        def _():
            child(b, q, remote).wait_send()

    base_copy = pltpu.make_async_copy(base_tiles.at[0, 0, 0], bbuf, bsem)

    @pl.when(owner)
    def _():
        base_copy.start()

    each(begin)
    wcopy.wait_recv()

    p_own = 2 * f + z
    for q in range(3):
        n = widths[q]

        @pl.when(f == q)
        def _(q=q, n=n):
            base_copy.wait()
            for s in range(4):
                pltpu.make_async_copy(packed.at[0, :, pl.ds(0, n)], cbuf.at[s, :, pl.ds(0, n)], csem.at[s]).wait()
            for col in range(2 * q + 2):
                v = bbuf[:, 128 * col:128 * col + 128]
                for g in range(2):
                    v = v + spread(wb, g, lambda c, g=g: cbuf[2 * g, :, 128 * c:128 * c + 128] + cbuf[2 * g + 1, :, 128 * c:128 * c + 128], col)
                top[p_own, :, 128 * col:128 * col + 128] = v

    def tile_copy(q, zz, send, recv, to):
        piece = (2 * q + zz, slice(None), pl.ds(0, 256 * q + 256))
        return pltpu.make_async_remote_copy(
            src_ref=top.at[piece], dst_ref=top.at[piece], send_sem=send, recv_sem=recv, device_id=to, device_id_type=MESH)

    mine = f % 4
    for q in range(3):
        @pl.when(mine == q)
        def _(q=q):
            @pl.when(y == 0)
            def _():
                for n, dy in enumerate((2, 1, 3)):
                    tile_copy(q, z, ssem.at[6 + n], ysem.at[0], at(0, dy, 0, 0)).start()

            @pl.when(y > 0)
            def _():
                tile_copy(q, z, ssem.at[6], ysem.at[0], at(0, 1, 0, 0)).wait_recv()

            for n, (dz, dx) in enumerate(((1, 1), (0, 1), (1, 0))):
                tile_copy(q, z, ssem.at[9 + n], xsem.at[2 * q + z], at(dz, 0, dx, 0)).start()
            tile_copy(q, z, ssem.at[(14 if q == 2 else 12) + z], ksem.at[2 * q + z], at(0, 0, 0, 1)).start()

    for q in range(3):
        @pl.when(k == q % 2)
        def _(q=q):
            for zz in range(2):
                @pl.when((mine != q) | (z != zz))
                def _(zz=zz):
                    tile_copy(q, zz, ssem.at[9], xsem.at[2 * q + zz], at(0, 0, 1, 0)).wait_recv()
                    tile_copy(q, zz, ssem.at[14 + zz if q == 2 else 12 + zz], ksem.at[2 * q + zz], at(0, 0, 0, 1)).start()
    for q in range(3):
        @pl.when(k != q % 2)
        def _(q=q):
            for zz in range(2):
                tile_copy(q, zz, ssem.at[9], ksem.at[2 * q + zz], at(0, 0, 0, 1)).wait_recv()

    wcopy.wait_send()
    each(sent)
    for q in range(3):
        @pl.when(mine == q)
        def _(q=q):
            @pl.when(y == 0)
            def _():
                for n in range(3):
                    tile_copy(q, z, ssem.at[6 + n], ysem.at[0], at(0, 1, 0, 0)).wait_send()

            for n in range(3):
                tile_copy(q, z, ssem.at[9 + n], xsem.at[2 * q + z], at(0, 0, 1, 0)).wait_send()

        @pl.when(k == q % 2)
        def _(q=q):
            for zz in range(2):
                tile_copy(q, zz, ssem.at[14 + zz if q == 2 else 12 + zz], ksem.at[2 * q + zz], at(0, 0, 0, 1)).wait_send()


def lead(packed, base_tiles, w):
    return pl.pallas_call(
        top_kernel,
        out_shape=(jax.ShapeDtypeStruct((6, 128, 768), jnp.float32), jax.ShapeDtypeStruct((2, 8, 128), jnp.float32)),
        in_specs=[ANY, ANY, VM],
        out_specs=(VM, VM),
        scratch_shapes=[
            pltpu.VMEM((4, 128, 512), jnp.float32),
            pltpu.VMEM((128, 768), jnp.float32),
            pltpu.SemaphoreType.DMA((16,)),
            pltpu.SemaphoreType.DMA((2,)),
            pltpu.SemaphoreType.DMA((4,)),
            pltpu.SemaphoreType.DMA,
            pltpu.SemaphoreType.DMA((1,)),
            pltpu.SemaphoreType.DMA((6,)),
            pltpu.SemaphoreType.DMA((6,)),
        ],
        compiler_params=pltpu.CompilerParams(collective_id=0, has_side_effects=True, vmem_limit_bytes=58 << 20),
        cost_estimate=pl.CostEstimate(flops=20_000_000_000, bytes_accessed=8_000_000, transcendentals=0),
        name="lead_gather",
    )(packed, base_tiles, w)


def finish_kernel(arr, base_ref, l_ref, m_ref, wb, o_ref):
    z = lax.axis_index("bit")
    f = lax.axis_index("front")
    j = pl.program_id(0)
    cols = []
    for col in range(6):
        v = base_ref[0, 0, 0, :, 128 * col:128 * col + 128]
        for g in range(2):
            v = v + spread(wb, g, lambda c, g=g: arr[g, 0, 0, :, 128 * c:128 * c + 128] + arr[g, 1, 0, :, 128 * c:128 * c + 128], col)
        cols.append(v)
    a = jnp.concatenate(cols, 1)
    for s in range(3):
        hi = 256 * s + 256
        o_ref[0, 0, 0, :, 256 * s:hi] = nt(a[:, :hi], m_ref[256 * s:hi, :hi])

    @pl.when((j == 0) & (f <= 2))
    def _():
        o_ref[0, 0, 0] = l_ref[pl.ds(pl.multiple_of((2 * f + z) * 128, 128), 128), :]


def finish(arrived, base_tiles, low, inv, wb):
    arr = arrived.reshape(2, 2, 8, 128, 512)
    full = pl.BlockSpec((768, 768), lambda j: (0, 0))
    return pl.pallas_call(
        finish_kernel,
        out_shape=jax.ShapeDtypeStruct((1, 1, 8, 128, 768), jnp.float32),
        grid=(8,),
        in_specs=[
            pl.BlockSpec((2, 2, 1, 128, 512), lambda j: (0, 0, j, 0, 0)),
            pl.BlockSpec((1, 1, 1, 128, 768), lambda j: (0, 0, j, 0, 0)),
            full,
            full,
            pl.BlockSpec((2, 8, 128), lambda j: (0, 0, 0)),
        ],
        out_specs=pl.BlockSpec((1, 1, 1, 128, 768), lambda j: (0, 0, j, 0, 0)),
        compiler_params=pltpu.CompilerParams(vmem_limit_bytes=40 << 20),
        name="finish_rows",
    )(arr, base_tiles, low, inv, wb)


def body(child_block, child_rows, child_cols, parent_base):
    f = lax.axis_index("front")
    dest = jnp.arange(32, dtype=jnp.int32)
    target = 32 * (f % 8) + 2 * (dest % 16) + dest // 16
    number = jnp.arange(1, 15, dtype=jnp.int32)
    pick = jnp.sum(jnp.where(child_rows[0, 0][None, :] == target[:, None], number[None, :], 0), axis=1)
    packed = pack(pick, child_block[0, 0])
    c1, c2 = child_cols[0, 1], child_cols[0, 2]
    masks = jnp.stack([c1 == 1, c1 == 2, c2 == 2, c1 == 3, c2 == 3, c2 == 4, c1 == 0, c1 == 0])
    w = jnp.broadcast_to(masks.astype(jnp.float32)[:, None], (8, 128))
    arrived = lax.all_to_all(packed, ("bit", "front"), split_axis=0, concat_axis=0, tiled=True)
    top, wb = lead(packed, parent_base, w)
    low, inv = chol(top.reshape(768, 768))
    return finish(arrived, parent_base, low, inv, wb)


def solution(mesh):
    mesh = Mesh(mesh.devices.reshape(4, 2, 16), ("pair", "bit", "front"))
    cube = ("pair", "bit")
    placed = (P(cube, "front"), P(cube, "front"), P(cube), P(cube, "front"))
    return jax.shard_map(body, mesh=mesh, in_specs=placed, out_specs=P(cube, "front"), check_vma=False)
```

time: 891 us -> 261 us (0.29)
  the two profiles are of different devices: /device:TPU:31 before, /device:TPU:105 now
where the time goes in v1:
time: 261 us; the launch traced here: 260 us
  Pallas kernels  237 us (91%)
  local copies, waits for them, and re-layouts  9.22 us (4%)
  starting transfers between devices  8.28 us (3%)
  between operations  4.51 us (2%)
    pallas_call x1, Pallas kernels, lead(): pl.pallas_call(top_kernel, out_shape=(jax.ShapeDtypeStruct((6, 128, 768),...  143 us
    pallas_call x1, Pallas kernels, chol(): pl.pallas_call(chol_kernel, out_shape=(s, s), in_specs=[VM], out_specs=(V...  59.1 us
    pallas_call x1, Pallas kernels, pack(): pl.pallas_call(pack_kernel, out_shape=jax.ShapeDtypeStruct((32, 128, 512)...  19 us
    pallas_call x1, Pallas kernels, finish(): pl.pallas_call(finish_kernel, out_shape=jax.ShapeDtypeStruct((1, 1, 8, 12...  15.8 us
    all_to_all x1, starting transfers between devices, body(): lax.all_to_all(packed, ('bit', 'front'), split_axis=0, concat_axis=0, til...  8.28 us
    unnamed x16, local copies, waits for them, and re-layouts  7.8 us
  transfers between devices with their start and end apart: 1, of which 0 were waited for; matrix products, arithmetic and copies ran while one was open for 1% of the time, Pallas kernels for 78%

profile of v1, /device:TPU:105, one launch (start us, length us, event | category | flops | bytes accessed | tf_op | source)
XLA Modules:
  0.0 259.8 jit_solution(2325632925787438161)
XLA Ops:
  0.0 1.3 select_reduce_fusion.pick
  1.3 19.0 %pack_tiles.1.packed = f32[32,128,512]{2,1,0:T(8,128)} custom-call(s32[32]{0:T(128)} %select_reduce_fusion.pick, f32[14,128,512]{2,1,0:T(8,128)} %bitcast.12), custom_call_target="tpu_custom_call" | custom-call | tf_op jit(solution)/shard_map/pack_tiles/pallas_call | solution.py:101
  20.3 0.0 copy-start.7
  20.3 8.3 %all-to-all-start = ((f32[32,128,512]{2,1,0:T(8,128)}), f32[32,128,512]{2,1,0:T(8,128)}, u32[]{:S(2)}, u32[]{:S(2)}) async-start(f32[32,128,512]{2,1,0:T(8,128)} %pack_tiles.1.packed), calls=%async_computation | async-start | bytes 16777216 | tf_op jit(solution)/shard_map/all_to_all | solution.py:334
  28.6 0.0 copy-done.7
  28.6 0.7 fusion.3
  33.7 0.1 stack.32
  33.8 0.7 broadcast_in_dim.22.w_in
  34.5 142.6 %lead_gather.1 = (f32[6,128,768]{2,1,0:T(8,128)}, f32[2,8,128]{2,1,0:T(8,128)}) custom-call(f32[32,128,512]{2,1,0:T(8,128)} %pack_tiles.1.packed, f32[1,1,8,128,768]{4,3,2,1,0:T(8,128)} %base_ref.1, f32[8,128]{1,0:T(8,128)} %broadcast_in_dim.22.w_in), custom_call_target="tpu_custom_call" | custom-call | flops 20000000000 | bytes 8000000 | tf_op jit(solution)/shard_map/lead_gather/pallas_call | solution.py:262
  177.1 0.0 copy-start.6
  177.1 1.7 copy-done.6
  178.7 0.0 copy-start
  178.7 0.0 copy-start.5
  178.7 59.1 %lead_factor.1 = (f32[768,768]{1,0:T(8,128)S(1)}, f32[768,768]{1,0:T(8,128)S(1)}) custom-call(f32[768,768]{1,0:T(8,128)S(1)} %bitcast.11), custom_call_target="tpu_custom_call" | custom-call | flops 40000000000 | bytes 8000000 | tf_op jit(solution)/shard_map/lead_factor/pallas_call | solution.py:82
  237.8 0.0 copy-start.1
  237.8 1.4 copy-done.1
  239.2 1.4 copy-done.3
  240.6 0.0 all-to-all-done
  240.6 0.0 copy-done
  240.6 0.0 copy-done.5
  240.6 0.0 copy-start.2
  240.6 1.7 copy-done.2
  242.3 1.7 copy-done.4
  244.0 15.8 %finish_rows.1 = f32[1,1,8,128,768]{4,3,2,1,0:T(8,128)} custom-call(f32[2,2,8,128,512]{4,3,2,1,0:T(8,128)} %bitcast.2.arr, f32[1,1,8,128,768]{4,3,2,1,0:T(8,128)S(1)} %copy-done, f32[768,768]{1,0:T(8,128)S(1)} %copy-done.2, f32[768,768]{1,0:T(8,128)S(1)} %copy-done.4, f32[2,8,128]{2,1,0:T(8,128)S(1)} %copy-done.5), custom_call_target="tpu_custom_call" | custom-call | tf_op jit(solution)/shard_map/finish_rows/pallas_call | solution.py:307
  (5 shorter events, 0.0 us)
Async XLA Ops:
  20.3 8.3 %copy-start.7 = (s32[1,4]{1,0:T(1,128)S(1)}, s32[1,4]{1,0:T(1,128)}, u32[]{:S(2)}) copy-start(s32[1,4]{1,0:T(1,128)} %param.6) | copy-start | bytes 52
  20.3 220.3 %all-to-all-start = ((f32[32,128,512]{2,1,0:T(8,128)}), f32[32,128,512]{2,1,0:T(8,128)}, u32[]{:S(2)}, u32[]{:S(2)}) async-start(f32[32,128,512]{2,1,0:T(8,128)} %pack_tiles.1.packed), calls=%async_computation | async-start | bytes 16777216 | tf_op jit(solution)/shard_map/all_to_all | solution.py:334
  177.1 1.7 copy-start.6
  178.7 61.9 %copy-start = (f32[1,1,8,128,768]{4,3,2,1,0:T(8,128)S(1)}, f32[1,1,8,128,768]{4,3,2,1,0:T(8,128)}, u32[]{:S(2)}) copy-start(f32[1,1,8,128,768]{4,3,2,1,0:T(8,128)} %base_ref.1) | copy-start | bytes 9437188
  178.7 61.9 %copy-start.5 = (f32[2,8,128]{2,1,0:T(8,128)S(1)}, f32[2,8,128]{2,1,0:T(8,128)}, u32[]{:S(2)}) copy-start(f32[2,8,128]{2,1,0:T(8,128)} %get-tuple-element.12.wb) | copy-start | bytes 24580
  237.8 1.4 copy-start.1
  239.2 1.4 copy-start.3
  240.6 1.7 copy-start.2
  242.3 1.7 copy-start.4
